TPU v7x, 128 devices: a whole 4x4x4 slice. The times are simulated.
128 devices in a mesh: utt: 4 (over x), tm: 4 (over y_hi, core), wshard: 8 (over y_lo, z).
Axes of the slice: x: 4, y: 4 (y_hi: 2, y_lo: 2; y = y_hi * 2 + y_lo), z: 4, core: 2. Of those that a mesh axis runs over, the one named last changes fastest.
Arguments:
- frames: bfloat16 [32, 2048, 1536], P(('utt', 'wshard'), 'tm'), may hold values from -6 to 6
- lengths: int32 [32], P(('utt', 'wshard')), may hold values from 512 to 2048, as said below
- cotangent: bfloat16 [32, 2048, 1536], P(('utt', 'wshard'), 'tm'), may hold values from -6 to 6
- norm_gain: float32 [1536], replicated, may hold values from 0.1 to 1.9
- w_in: bfloat16 [1536, 3072], P(('tm', 'wshard')), may hold values from -0.15625 to 0.15625
- kernel: float32 [31, 1536], replicated, may hold values from -1 to 1
- mid_gain: float32 [1536], replicated, may hold values from 0.1 to 1.9
- w_out: bfloat16 [1536, 1536], P(('tm', 'wshard')), may hold values from -0.15625 to 0.15625
Outputs:
- mixed: bfloat16 [32, 2048, 1536], P(('utt', 'wshard'), 'tm')
- grad_frames: bfloat16 [32, 2048, 1536], P(('utt', 'wshard'), 'tm')
- grad_in: float32 [1536, 3072], P(('tm', 'wshard'))
- grad_out: float32 [1536, 1536], P(('tm', 'wshard'))
- grad_kernel: float32 [31, 1536], replicated
- grad_norm_gain: float32 [1536], replicated
- grad_mid_gain: float32 [1536], replicated
Inputs may be any that keep to these rules, and one draw needn't show every extreme that they name: `lengths`: frames at or after an utterance's length are padding.
All inputs are finite; a program needn't handle non-finite values.
Results may differ from a plain program's by a relative error of at most 0.029.
Values may be sent and summed in bfloat16 or wider, within the bound.
A program may use at most 128 MiB of HBM per device.

v0:
```python
import functools
import math

import jax
import jax.numpy as jnp
from jax import lax
from jax.experimental import pallas as pl
from jax.experimental.pallas import tpu as pltpu
from jax.sharding import PartitionSpec as P

EPS = 1e-05
MESH = pl.DeviceIdType.MESH
F32 = jnp.float32
BF16 = jnp.bfloat16
ROWS = 48
D = 1536
FRAMES = 512
HALF = D // 2


def around(value, shift):
    return lax.rem(value + shift, 4)


class Place:
    def __init__(self):
        tm, ws = lax.axis_index("tm"), lax.axis_index("wshard")
        self.x = lax.axis_index("utt")
        self.c = lax.rem(tm, 2)
        self.y = lax.div(tm, 2) * 2 + lax.div(ws, 4)
        self.z = lax.rem(ws, 4)

    def device(self, x, y, z, c):
        return (x, lax.div(y, 2) * 2 + c, lax.rem(y, 2) * 4 + z)

    def at(self, axis, shift):
        x, y, z = self.x, self.y, self.z
        if axis == "x":
            x = around(x, shift)
        if axis == "y":
            y = around(y, shift)
        if axis == "z":
            z = around(z, shift)
        return self.device(x, y, z, self.c)

    def sibling(self):
        return self.device(self.x, self.y, self.z, 1 - self.c)

    def greet(self):
        barrier = pltpu.get_barrier_semaphore()
        others = [self.at(axis, shift) for axis in "xyz" for shift in (1, 2, 3)]
        others.append(self.sibling())
        others.append(self.device(self.x, around(self.y, 2), self.z, 1 - self.c))
        for other in others:
            pl.semaphore_signal(barrier, inc=1, device_id=other, device_id_type=MESH)
        pl.semaphore_wait(barrier, len(others))


class Net:
    def __init__(self, place, sent, landed):
        self.place, self.sent, self.landed = place, sent, landed
        self.count = 0
        self.flying = {}

    def send(self, src, dst, device):
        slot = self.count
        self.count += 1
        copy = pltpu.make_async_remote_copy(
            src_ref=src,
            dst_ref=dst,
            send_sem=self.sent.at[slot],
            recv_sem=self.landed.at[slot],
            device_id=device,
            device_id_type=MESH,
        )
        copy.start()
        self.flying[slot] = copy
        return slot

    def wait(self, slot, dst):
        pltpu.make_async_remote_copy(
            src_ref=dst,
            dst_ref=dst,
            send_sem=self.sent.at[slot],
            recv_sem=self.landed.at[slot],
            device_id=self.place.sibling(),
            device_id_type=MESH,
        ).wait_recv()

    def gone(self, slots):
        for slot in slots:
            self.flying.pop(slot).wait_send()

    def drain(self):
        self.gone(list(self.flying))


class Gather:
    def __init__(self, net, place, full):
        self.net, self.place, self.full = net, place, full
        self.portion = full.shape[-1] // 3
        self.quarter = self.portion // 4

    def part_a(self, dy, dz):
        p = self.place
        y = around(p.y, 4 - dy)
        z = around(p.z, 4 - dz)
        return self.full.at[p.c, y, z, :, pl.ds(0, self.portion)]

    def part_b(self, dy, dz):
        p = self.place
        y = around(p.y, 4 - dy)
        z = around(p.z, 4 - dz)
        return self.full.at[p.c, y, z, :, pl.ds(self.portion, self.portion)]

    def columns(self, which, dx):
        x = around(self.place.x, 4 - dx)
        start = pl.multiple_of(which * self.portion + x * self.quarter, 128)
        return pl.ds(start, self.quarter)

    def quarter_b(self, dy, dx):
        p = self.place
        return self.full.at[p.c, around(p.y, 4 - dy), p.z, :, self.columns(1, dx)]

    def quarter_c(self, dy, dz, dx):
        p = self.place
        return self.full.at[
            p.c, around(p.y, 4 - dy), around(p.z, 4 - dz), :, self.columns(2, dx)
        ]

    def group_c(self, group, dx):
        p = self.place
        dy, dz = group
        if dz is None:
            return self.full.at[p.c, around(p.y, 4 - dy), :, :, self.columns(2, dx)]
        return self.quarter_c(dy, dz, dx)

    def share(self, name, c):
        p = self.place
        kind, shift = name
        if kind == "a":
            return self.full.at[c, around(p.y, 4 - shift), :, :, pl.ds(0, self.portion)]
        if kind == "b":
            return self.full.at[
                c, :, around(p.z, 4 - shift), :, pl.ds(self.portion, self.portion)
            ]
        return self.full.at[c, :, :, :, self.columns(2, shift)]

    def give(self, name):
        ref = self.share(name, self.place.c)
        self.shared.append((name, self.net.send(ref, ref, self.place.sibling())))

    def begin(self):
        net, p = self.net, self.place
        self.shared = []
        own_b, own_c = self.quarter_b(0, 0), self.quarter_c(0, 0, 0)
        own_a, own_whole_b = self.part_a(0, 0), self.part_b(0, 0)
        self.c_z, self.b_y, self.a_z = {}, {}, {}
        self.c_y, self.a_y, self.b_z = {}, {}, {}
        self.c_x, self.b_x = {}, {}
        for shift in (1, 3, 2):
            self.c_z[shift] = net.send(own_c, own_c, p.at("z", shift))
            self.b_y[shift] = net.send(own_b, own_b, p.at("y", shift))
        for shift in (1, 3, 2):
            self.a_z[shift] = net.send(own_a, own_a, p.at("z", shift))
            self.c_y[shift, 0] = net.send(own_c, own_c, p.at("y", shift))
        for shift in (1, 3):
            self.a_y[shift, 0] = net.send(own_a, own_a, p.at("y", shift))
            self.b_z[shift, 0] = net.send(own_whole_b, own_whole_b, p.at("z", shift))

    def second(self):
        net, p = self.net, self.place
        for d in (1, 3, 2):
            ref = self.quarter_c(0, d, 0)
            net.wait(self.c_z[d], ref)
            for shift in (1, 3, 2):
                self.c_y[shift, d] = net.send(ref, ref, p.at("y", shift))
            for shift in (1, 3):
                self.c_x[shift, (0, d)] = net.send(ref, ref, p.at("x", shift))
            ref = self.quarter_b(d, 0)
            net.wait(self.b_y[d], ref)
            for shift in (1, 3, 2):
                self.b_x[shift, d] = net.send(ref, ref, p.at("x", shift))
        for d in (1, 3, 2):
            ref = self.part_a(0, d)
            net.wait(self.a_z[d], ref)
            for shift in (1, 3):
                self.a_y[shift, d] = net.send(ref, ref, p.at("y", shift))
        self.give(("a", 0))

    def third(self):
        net, p = self.net, self.place
        for d in (1, 3, 2):
            for shift in (1, 3, 2):
                net.wait(self.b_x[shift, d], self.quarter_b(d, shift))
            ref = self.part_b(d, 0)
            for shift in (1, 3):
                self.b_z[shift, d] = net.send(ref, ref, p.at("z", shift))
            for dz in range(4):
                net.wait(self.c_y[d, dz], self.quarter_c(d, dz, 0))
            ref = self.group_c((d, None), 0)
            for shift in (1, 3):
                self.c_x[shift, (d, None)] = net.send(ref, ref, p.at("x", shift))
        self.give(("b", 0))
        self.give(("c", 0))

    def onward(self, table, keys, region, axis):
        net, p = self.net, self.place
        far = {}
        for number, key in enumerate(keys):
            for shift in (1, 3):
                ref = region(key, shift)
                net.wait(table[shift, key], ref)
                if (number % 2 == 0) == (shift == 1):
                    far[key] = net.send(ref, ref, p.at(axis, shift))
        return far

    def fourth(self):
        groups = [(0, 1), (0, 3), (0, 2), (1, None), (3, None), (2, None)]
        self.groups = groups
        self.a_far = self.onward(self.a_y, (0, 1, 3, 2), lambda d, s: self.part_a(s, d), "y")
        self.b_far = self.onward(self.b_z, (0, 1, 3, 2), lambda d, s: self.part_b(d, s), "z")
        self.c_far = self.onward(self.c_x, groups, lambda g, s: self.group_c(g, s), "x")
        for shift in (1, 3):
            for kind in "abc":
                self.give((kind, shift))

    def finish(self):
        net, p = self.net, self.place
        for d in (0, 1, 3, 2):
            net.wait(self.a_far[d], self.part_a(2, d))
        self.give(("a", 2))
        for d in (0, 1, 3, 2):
            net.wait(self.b_far[d], self.part_b(d, 2))
        self.give(("b", 2))
        for group in self.groups:
            net.wait(self.c_far[group], self.group_c(group, 2))
        self.give(("c", 2))
        for name, slot in self.shared:
            net.wait(slot, self.share(name, 1 - p.c))


GATHER_COPIES = 90


def add_into(target, term):
    target[...] = (target[...].astype(F32) + term[...].astype(F32)).astype(target.dtype)


class Scatter:
    def __init__(self, net, place, terms, bufs):
        self.net, self.place, self.terms = net, place, terms
        self.portion = terms.shape[-1] // 3
        self.quarter = self.portion // 4
        self.near, self.mid, self.final, self.done = bufs
        self.slots = {}

    @staticmethod
    def scratch(columns):
        portion, quarter = columns // 3, columns // 12
        return [
            [
                pltpu.VMEM((2, 2, ROWS, portion), BF16),
                pltpu.VMEM((2, 2, ROWS, portion), BF16),
                pltpu.VMEM((2, 2, 4, ROWS, quarter), BF16),
                pltpu.VMEM((2, 4, ROWS, portion), BF16),
                pltpu.VMEM((2, 4, ROWS, portion), BF16),
                pltpu.VMEM((2, 4, 4, ROWS, quarter), BF16),
            ],
            [
                pltpu.VMEM((3, ROWS, portion), BF16),
                pltpu.VMEM((3, 4, ROWS, quarter), BF16),
                pltpu.VMEM((3, 4, ROWS, quarter), BF16),
            ],
            [pltpu.VMEM((3, ROWS, quarter), BF16)] * 3,
            pltpu.VMEM((4, 3, ROWS, quarter), BF16),
        ]

    def columns(self, which, x):
        start = pl.multiple_of(which * self.portion + x * self.quarter, 128)
        return pl.ds(start, self.quarter)

    def whole(self, which):
        return pl.ds(which * self.portion, self.portion)

    def first(self, which, shift, half=None):
        p, of = self.place, self.terms
        part = slice(None) if half is None else pl.ds(2 * half, 2)
        if which == 0:
            return of.at[around(p.y, shift), part, :, self.whole(0)]
        if which == 1:
            return of.at[part, around(p.z, shift), :, self.whole(1)]
        return of.at[part, :, :, self.columns(2, around(p.x, shift))]

    def second(self, which, shift):
        p, mine = self.place, self.terms
        if which == 0:
            return mine.at[p.y, around(p.z, shift), :, self.whole(0)]
        if which == 1:
            return mine.at[:, p.z, :, self.columns(1, around(p.x, shift))]
        return mine.at[around(p.y, shift), :, :, self.columns(2, p.x)]

    def third(self, which, shift):
        p, mine = self.place, self.terms
        if which == 0:
            return mine.at[p.y, p.z, :, self.columns(0, around(p.x, shift))]
        if which == 1:
            return mine.at[around(p.y, shift), p.z, :, self.columns(1, p.x)]
        return mine.at[p.y, around(p.z, shift), :, self.columns(2, p.x)]

    AXES = (("y", "z", "x"), ("z", "x", "y"), ("x", "y", "z"))

    def step_far(self):
        net, p = self.net, self.place
        for which in range(3):
            axis = self.AXES[which][0]
            for half, shift in ((0, 1), (1, 3)):
                self.slots["far", which, half] = net.send(
                    self.first(which, 2, half),
                    self.near[which].at[half],
                    p.at(axis, shift),
                )

    def step_near(self):
        net, p = self.net, self.place
        for which in range(3):
            axis = self.AXES[which][0]
            for half, shift in ((0, 1), (1, 3)):
                came = self.near[which].at[half]
                net.wait(self.slots["far", which, half], came)
                target = self.first(which, shift, half)
                for i in range(2):
                    add_into(target.at[i], came.at[i])
                self.slots["near", which, half] = net.send(
                    self.first(which, shift),
                    self.near[3 + which].at[half],
                    p.at(axis, shift),
                )

    def step_second(self):
        net, p = self.net, self.place
        for which in range(3):
            axis = self.AXES[which][1]
            target = self.first(which, 0)
            for half in range(2):
                came = self.near[3 + which].at[half]
                net.wait(self.slots["near", which, half], came)
                for i in range(4):
                    add_into(target.at[i], came.at[i])
            for shift in (2, 1, 3):
                self.slots["second", which, shift] = net.send(
                    self.second(which, shift), self.mid[which].at[shift - 1], p.at(axis, shift)
                )

    def step_third(self):
        net, p = self.net, self.place
        for which in range(3):
            axis = self.AXES[which][2]
            target = self.second(which, 0)
            for shift in (1, 3, 2):
                came = self.mid[which].at[shift - 1]
                net.wait(self.slots["second", which, shift], came)
                if which == 0:
                    add_into(target, came)
                else:
                    for i in range(4):
                        add_into(target.at[i], came.at[i])
            for shift in (2, 1, 3):
                self.slots["third", which, shift] = net.send(
                    self.third(which, shift), self.final[which].at[shift - 1], p.at(axis, shift)
                )

    def step_spread(self):
        net, p = self.net, self.place
        for which in range(3):
            total = self.third(which, 0)[...].astype(F32)
            for shift in (1, 3, 2):
                came = self.final[which].at[shift - 1]
                net.wait(self.slots["third", which, shift], came)
                total = total + came[...].astype(F32)
            self.done[p.x, which] = total.astype(BF16)
        for shift in (2, 1, 3):
            self.slots["spread", shift] = net.send(
                self.done.at[p.x], self.done.at[p.x], p.at("x", shift)
            )

    def step_last(self, store):
        net, p = self.net, self.place
        for shift in (1, 3, 2):
            net.wait(self.slots["spread", shift], self.done.at[around(p.x, 4 - shift)])
        for which in range(3):
            for x in range(4):
                store(which * self.portion + x * self.quarter, self.done[x, which].astype(F32))


SCATTER_COPIES = 33


class Total:
    ORDERS = ("xyz", "yzx", "zxy")

    def __init__(self, net, place, terms, pair, stages, out):
        self.net, self.place, self.terms, self.pairbuf = net, place, terms, pair
        self.stages, self.out = stages, out
        self.slots = {}

    @staticmethod
    def scratch(rows, width):
        return [
            pltpu.VMEM((3, rows, width), F32),
            pltpu.VMEM((3, 3, 4, rows, width), F32),
        ]

    def coordinate(self, axis):
        return {"x": self.place.x, "y": self.place.y, "z": self.place.z}[axis]

    def to_sibling(self):
        p = self.place
        self.slots["pair"] = self.net.send(self.terms.at[1 - p.c], self.pairbuf, p.sibling())

    def put(self, stage, portion, value):
        axis = self.ORDERS[portion][stage]
        own = self.stages.at[stage, portion, self.coordinate(axis)]
        own[...] = value
        for shift in (2, 1, 3):
            self.slots[stage, portion, shift] = self.net.send(own, own, self.place.at(axis, shift))

    def begin(self):
        self.net.wait(self.slots["pair"], self.pairbuf)
        for portion in range(3):
            self.put(0, portion, self.terms[self.place.c, portion] + self.pairbuf[portion])

    def collect(self, stage, portion):
        axis = self.ORDERS[portion][stage]
        for shift in (1, 3, 2):
            other = around(self.coordinate(axis), 4 - shift)
            self.net.wait(self.slots[stage, portion, shift], self.stages.at[stage, portion, other])
        s = self.stages
        return (s[stage, portion, 0] + s[stage, portion, 1]) + (
            s[stage, portion, 2] + s[stage, portion, 3]
        )

    def step(self, stage):
        for portion in range(3):
            self.put(stage, portion, self.collect(stage - 1, portion))

    def spread(self):
        p = self.place
        for portion in range(3):
            self.out[p.c, portion] = self.collect(2, portion)
        self.slots["back"] = self.net.send(self.out.at[p.c], self.out.at[p.c], p.sibling())

    def last(self):
        self.net.wait(self.slots["back"], self.out.at[1 - self.place.c])


TOTAL_COPIES = 32


def swapped(value):
    return jnp.concatenate(
        [value[:, :384], value[:, 768:1152], value[:, 384:768], value[:, 1152:]], axis=1
    )


def rows_of(i, size):
    return pl.ds(pl.multiple_of(i * size, size), size)


def valid_rows(length, first, start, rows):
    position = first + start + lax.broadcasted_iota(jnp.int32, (rows, 1), 0)
    return (position < length).astype(F32)


def norm_stage(first, last, frames, gain, normed, mean_ref, inverse_ref):
    @pl.loop(first, last)
    def _(i):
        rows = rows_of(i, 32)
        value = frames[rows, :].astype(F32)
        mean = jnp.mean(value, -1, keepdims=True)
        center = value - mean
        inverse = lax.rsqrt(jnp.mean(center * center, -1, keepdims=True) + EPS)
        mean_ref[rows, :] = mean
        inverse_ref[rows, :] = inverse
        normed[rows, :] = swapped((center * inverse * gain[...]).astype(BF16))


def hidden_stage(first, last, normed, in_full, linear, opened, padded, valid):
    @pl.loop(first, last)
    def _(j):
        for half in range(2):
            rows = pl.ds(half * 256, 256)
            left = normed[rows, :]
            low = pl.ds(pl.multiple_of(j * 256, 256), 256)
            high = pl.ds(pl.multiple_of(D + j * 256, 256), 256)
            lin = jnp.dot(
                left, in_full[:, :, :, :, low].reshape(D, 256), preferred_element_type=F32
            )
            gate = jnp.dot(
                left, in_full[:, :, :, :, high].reshape(D, 256), preferred_element_type=F32
            )
            gate = jax.nn.sigmoid(gate)
            linear[rows, low] = lin.astype(BF16)
            opened[rows, low] = gate.astype(BF16)
            gated = (lin * gate * valid(half * 256, 256)).astype(BF16).astype(F32)
            inside = pl.ds(16 + half * 256, 256)
            padded[2 * j, inside, :] = gated[:, :128]
            padded[2 * j + 1, inside, :] = gated[:, 128:]


def taps_sum(source, i, base, tap):
    total = None
    for r in range(8):
        window = source[i, pl.ds(base + r + 1, 152), :]
        for j in range(4):
            k = 8 * j + r
            if k < 31:
                term = tap(k) * window[8 * j : 8 * j + 128]
                total = term if total is None else total + term
    return total


def conv_stage(bases, padded, taps, temporal):
    @pl.loop(0, 12)
    def _(i):
        for base in bases:
            total = taps_sum(padded, i, base, lambda k: taps[i, k : k + 1, :])
            temporal[pl.ds(base, 128), pl.ds(pl.multiple_of(i * 128, 128), 128)] = total


def mid_stage(temporal, gain, smooth_grad, smooth, grad_padded, mid_term):
    mid_term[...] = jnp.zeros_like(mid_term)

    @pl.loop(0, 16)
    def _(i):
        rows = rows_of(i, 32)
        value = temporal[rows, :]
        mean = jnp.mean(value, -1, keepdims=True)
        center = value - mean
        inverse = lax.rsqrt(jnp.mean(center * center, -1, keepdims=True) + EPS)
        hat = center * inverse
        scaled = hat * gain[...]
        s = jax.nn.sigmoid(scaled)
        smooth[rows, :] = swapped((scaled * s).astype(BF16))
        grad = smooth_grad[rows, :].astype(F32) * (s * (1.0 + scaled * (1.0 - s)))
        mid_term[...] += jnp.sum((grad * hat).reshape(4, 8, D), 0)
        q = grad * gain[...]
        result = inverse * (
            q - jnp.mean(q, -1, keepdims=True) - hat * jnp.mean(q * hat, -1, keepdims=True)
        )
        result = result.astype(BF16).astype(F32)
        inside = pl.ds(pl.multiple_of(16 + i * 32, 16), 32)
        for t in range(12):
            grad_padded[t, inside, :] = result[:, t * 128 : (t + 1) * 128]


def backward_conv(first, last, padded, grad_padded, taps, linear, opened, valid, hidden_grad, sums):
    @pl.loop(first, last)
    def _(i):
        columns = pl.ds(pl.multiple_of(i * 128, 128), 128)
        high = pl.ds(pl.multiple_of(D + i * 128, 128), 128)
        for base in range(0, 512, 128):
            rows = pl.ds(base, 128)
            grad = taps_sum(grad_padded, i, base, lambda k: taps[i, 30 - k : 31 - k, :])
            grad = grad * valid(base, 128)
            gate = opened[rows, columns].astype(F32)
            direct = grad * gate
            hidden_grad[rows, columns] = direct.astype(BF16)
            hidden_grad[rows, high] = (
                direct * linear[rows, columns].astype(F32) * (1.0 - gate)
            ).astype(BF16)
            here = grad_padded[i, pl.ds(base + 16, 128), :]
            for r in range(8):
                window = padded[i, pl.ds(base + r + 1, 152), :]
                for j in range(4):
                    k = 8 * j + r
                    if k < 31:
                        term = (window[8 * j : 8 * j + 128] * here).reshape(16, 8, 128)
                        term = jnp.sum(term, 0)
                        if base:
                            sums[i, k] += term
                        else:
                            sums[i, k] = term


def transposed_product(left, right):
    return lax.dot_general(
        left, right, (((1,), (1,)), ((), ())), preferred_element_type=F32
    )


def transpose_stage(source, own, other, c):
    for half, target in ((c, own), (1 - c, other)):

        @pl.loop(0, 6)
        def _(j):
            columns = pl.ds(pl.multiple_of(half * HALF + j * 128, 128), 128)
            for base in range(0, FRAMES, 128):
                block = source[pl.ds(base, 128), columns]
                target[rows_of(j, 128), pl.ds(base, 128)] = jnp.transpose(block)


def weight_grad(left, right, right_column, target, target_column):
    @pl.loop(0, 6)
    def _(t):
        value = jnp.dot(
            left[...],
            right[:, pl.ds(pl.multiple_of(right_column(t), 256), 256)],
            preferred_element_type=F32,
        )
        target[:, :, :, pl.ds(pl.multiple_of(target_column(t), 256), 256)] = (
            value.astype(BF16).reshape(4, 4, ROWS, 256)
        )


def back_product(parts, left, full, result):
    for q in parts:
        yh, c = q // 2, q % 2
        weights = full[c, 2 * yh : 2 * yh + 2].reshape(384, full.shape[-1])
        result[:, q * 384 : (q + 1) * 384] = transposed_product(left[...], weights).astype(
            result.dtype
        )


def branch_stage(smooth, out_full, frames, valid, mixed):
    @pl.loop(0, 6)
    def _(j):
        columns = rows_of(j, 256)
        value = jnp.dot(
            smooth[...],
            out_full[:, :, :, :, columns].reshape(D, 256),
            preferred_element_type=F32,
        )
        mixed[:, columns] = (frames[:, columns].astype(F32) + valid(0, 512) * value).astype(BF16)


def frames_stage(frames, cotangent, gain, mean_ref, inverse_ref, normed_grad, result, in_term):
    in_term[...] = jnp.zeros_like(in_term)

    @pl.loop(0, 16)
    def _(i):
        rows = rows_of(i, 32)
        inverse = inverse_ref[rows, :]
        centred = (frames[rows, :].astype(F32) - mean_ref[rows, :]) * inverse
        grad = normed_grad[rows, :]
        in_term[...] += jnp.sum((grad * centred).reshape(4, 8, D), 0)
        p = grad * gain[...]
        change = inverse * (
            p - jnp.mean(p, -1, keepdims=True) - centred * jnp.mean(p * centred, -1, keepdims=True)
        )
        result[rows, :] = (cotangent[rows, :].astype(F32) + change).astype(BF16)


def edges(net, place, padded):
    tm = lax.axis_index("tm")
    rows = {"first": padded.at[:, 16:32, :], "last": padded.at[:, FRAMES : FRAMES + 16, :]}
    before, after = padded.at[:, 0:16, :], padded.at[:, FRAMES + 16 : FRAMES + 32, :]
    here = (lax.axis_index("utt"), lax.axis_index("wshard"))
    ahead = (here[0], around(tm, 1), here[1])
    behind = (here[0], around(tm, 3), here[1])
    slots = (net.send(rows["last"], before, ahead), net.send(rows["first"], after, behind))

    def arrive():
        net.wait(slots[0], before)
        net.wait(slots[1], after)
        padded[:, 0:16, :] = padded[:, 0:16, :] * (tm > 0).astype(F32)
        padded[:, FRAMES + 16 : FRAMES + 32, :] = padded[:, FRAMES + 16 : FRAMES + 32, :] * (
            tm < 3
        ).astype(F32)

    return arrive


def module_kernel(scale, tree, *refs):
    (
        length_ref, frames_hbm, cotangent_hbm, norm_gain, in_hbm, taps, mid_gain, out_hbm,
        mixed_hbm, grad_frames_hbm, grad_in, grad_out, grad_taps, grad_norm_gain, grad_mid_gain,
    ) = refs[:15]
    (
        in_full, out_full, frames, branch_grad, normed, smooth, linear, opened, padded, grad_padded,
        temporal, smooth_grad, hidden_grad, normed_t, smooth_t, other_t, mean_ref, inverse_ref,
        sums, mid_term, in_term, first_terms, second_terms, small, small_sum,
        sent, landed, local, bufs,
    ) = jax.tree_util.tree_unflatten(tree, refs[15:])
    place = Place()
    net = Net(place, sent, landed)
    c = place.c
    sibling = place.sibling()
    length = length_ref[0]
    start = lax.axis_index("tm") * FRAMES

    def valid(first, rows):
        return valid_rows(length, start, first, rows)

    loads = [
        pltpu.make_async_copy(in_hbm, in_full.at[c, place.y, place.z], local.at[0]),
        pltpu.make_async_copy(frames_hbm, frames, local.at[1]),
        pltpu.make_async_copy(cotangent_hbm, branch_grad.at[0:FRAMES], local.at[2]),
        pltpu.make_async_copy(out_hbm, out_full.at[c, place.y, place.z], local.at[3]),
    ]
    for load in loads:
        load.start()
    place.greet()
    gather_in, gather_out = Gather(net, place, in_full), Gather(net, place, out_full)
    loads[0].wait()
    gather_in.begin()
    loads[1].wait()
    norm = (frames, norm_gain, normed, mean_ref, inverse_ref)
    norm_stage(0, 6, *norm)
    gather_in.second()
    norm_stage(6, 16, *norm)
    gather_in.third()
    loads[2].wait()

    @pl.loop(0, 8)
    def _(i):
        rows = rows_of(i, 64)
        branch_grad[rows, :] = (branch_grad[rows, :].astype(F32) * valid(i * 64, 64)).astype(BF16)

    pair_branch = net.send(branch_grad.at[0:FRAMES], branch_grad.at[FRAMES : 2 * FRAMES], sibling)
    transpose_stage(normed, normed_t.at[:, 0:FRAMES], other_t, c)
    pair_normed = net.send(other_t, normed_t.at[:, FRAMES : 2 * FRAMES], sibling)
    gather_in.fourth()
    loads[3].wait()
    out_first = net.count
    gather_out.begin()
    gather_in.finish()
    gather_out.second()
    hidden = (normed, in_full, linear, opened, padded, valid)
    hidden_stage(0, 3, *hidden)
    gather_out.third()
    hidden_stage(3, 6, *hidden)
    arrive = edges(net, place, padded)
    gather_out.fourth()
    conv_stage((128, 256), padded, taps, temporal)
    arrive()
    conv_stage((0, 384), padded, taps, temporal)
    gather_out.finish()
    out_last = net.count
    back_product(range(4), branch_grad.at[0:FRAMES], out_full, smooth_grad)
    mid_stage(temporal, mid_gain, smooth_grad, smooth, grad_padded, mid_term)
    arrive = edges(net, place, grad_padded)

    net.gone([pair_normed])
    transpose_stage(smooth, smooth_t.at[:, 0:FRAMES], other_t, c)
    pair_smooth = net.send(other_t, smooth_t.at[:, FRAMES : 2 * FRAMES], sibling)
    arrive()
    conv = (padded, grad_padded, taps, linear, opened, valid, hidden_grad, sums)
    pair_hidden = []

    def backward(group):
        backward_conv(2 * group, 2 * group + 2, *conv)
        for column in (256 * group, D + 256 * group):
            own = hidden_grad.at[0:FRAMES, column : column + 256]
            there = hidden_grad.at[FRAMES : 2 * FRAMES, column : column + 256]
            pair_hidden.append((net.send(own, there, sibling), there))

    def hidden_arrive():
        while pair_hidden:
            net.wait(*pair_hidden.pop(0))

    backward(0)
    net.wait(pair_branch, branch_grad.at[FRAMES : 2 * FRAMES])
    net.wait(pair_smooth, smooth_t.at[:, FRAMES : 2 * FRAMES])
    weight_grad(smooth_t, branch_grad, lambda t: t * 256, first_terms, lambda t: t * 256)
    scatter_out = Scatter(net, place, first_terms, bufs[0])
    scatter_out.step_far()
    backward(1)
    backward(2)
    scatter_out.step_near()
    net.wait(pair_normed, normed_t.at[:, FRAMES : 2 * FRAMES])
    hidden_arrive()

    def grad_half(half, target):
        weight_grad(
            normed_t,
            hidden_grad,
            lambda t: lax.rem(t, 2) * D + half * HALF + lax.div(t, 2) * 256,
            target,
            lambda t: lax.rem(t, 2) * HALF + lax.div(t, 2) * 256,
        )

    grad_half(0, second_terms)
    scatter_one = Scatter(net, place, second_terms, bufs[1])
    scatter_one.step_far()
    scatter_out.step_second()
    backward(3)
    scatter_out.step_third()
    backward(4)
    scatter_one.step_near()
    backward(5)
    scatter_out.step_spread()
    branch_stage(smooth, out_full, frames, valid, normed)
    store_mixed = pltpu.make_async_copy(normed, mixed_hbm, local.at[0])
    store_mixed.start()
    scatter_one.step_second()
    hidden_arrive()
    net.gone(range(out_first, out_last))
    third_terms = out_full.at[0]
    grad_half(1, third_terms)
    scatter_two = Scatter(net, place, third_terms, bufs[2])
    scatter_two.step_far()
    scatter_one.step_third()
    reload = pltpu.make_async_copy(cotangent_hbm, opened, local.at[1])
    reload.start()

    def store_out(column, value):
        grad_out[:, column : column + 128] = value * scale

    def store_in(half):
        def store(column, value):
            to = half * HALF + column + (HALF if column >= HALF else 0)
            grad_in[:, to : to + 128] = value * scale

        return store

    own_hidden = hidden_grad.at[0:FRAMES]
    back_product((0, 1), own_hidden, in_full, temporal)
    scatter_two.step_near()
    back_product((2, 3), own_hidden, in_full, temporal)
    scatter_two.step_second()
    reload.wait()
    frames_stage(
        frames, opened, norm_gain, mean_ref, inverse_ref, temporal, smooth, in_term
    )
    store_frames = pltpu.make_async_copy(smooth, grad_frames_hbm, local.at[2])
    store_frames.start()
    for i in range(12):
        lanes = slice((i % 2) * 128, (i % 2) * 128 + 128)
        columns = slice(i * 128, i * 128 + 128)
        core, portion = (i // 2) % 2, i // 4
        small[core, portion, 0:31, lanes] = jnp.sum(sums[i], 1)[0:31]
        small[core, portion, 31:32, lanes] = jnp.sum(in_term[:, columns], 0, keepdims=True)
        small[core, portion, 32:33, lanes] = jnp.sum(mid_term[:, columns], 0, keepdims=True)
        small[core, portion, 33:40, lanes] = jnp.zeros((7, 128), F32)
    total = Total(net, place, small, *bufs[3], small_sum)
    total.to_sibling()
    scatter_two.step_third()
    total.begin()
    scatter_one.step_spread()
    scatter_out.step_last(store_out)
    total.step(1)
    scatter_two.step_spread()
    total.step(2)
    scatter_one.step_last(store_in(0))
    total.spread()
    scatter_two.step_last(store_in(1))
    total.last()
    for core in range(2):
        for portion in range(3):
            columns = slice(portion * 512 + core * 256, portion * 512 + core * 256 + 256)
            grad_taps[:, columns] = small_sum[core, portion, 0:31, :] * scale
            grad_norm_gain[:, columns] = small_sum[core, portion, 31:32, :] * scale
            grad_mid_gain[:, columns] = small_sum[core, portion, 32:33, :] * scale
    store_mixed.wait()
    store_frames.wait()
    net.drain()


def body(frames, lengths, cotangent, norm_gain, w_in, kernel, mid_gain, w_out):
    scale = 1.0 / math.sqrt(
        FRAMES * lax.axis_size("utt") * lax.axis_size("tm") * lax.axis_size("wshard")
    )
    taps = jnp.pad(kernel, ((0, 1), (0, 0))).reshape(32, 12, 128).swapaxes(0, 1)
    block = (FRAMES, D)
    copies = 2 * GATHER_COPIES + 3 * SCATTER_COPIES + TOTAL_COPIES + 32
    scratch = [
        pltpu.VMEM((2, 4, 4, ROWS, 2 * D), BF16),
        pltpu.VMEM((2, 4, 4, ROWS, D), BF16),
        pltpu.VMEM(block, BF16),
        pltpu.VMEM((2 * FRAMES, D), BF16),
        pltpu.VMEM(block, BF16),
        pltpu.VMEM(block, BF16),
        pltpu.VMEM(block, BF16),
        pltpu.VMEM(block, BF16),
        pltpu.VMEM((12, FRAMES + 32, 128), F32),
        pltpu.VMEM((12, FRAMES + 32, 128), F32),
        pltpu.VMEM(block, F32),
        pltpu.VMEM(block, BF16),
        pltpu.VMEM((2 * FRAMES, 2 * D), BF16),
        pltpu.VMEM((HALF, 2 * FRAMES), BF16),
        pltpu.VMEM((HALF, 2 * FRAMES), BF16),
        pltpu.VMEM((HALF, FRAMES), BF16),
        pltpu.VMEM((FRAMES, 1), F32),
        pltpu.VMEM((FRAMES, 1), F32),
        pltpu.VMEM((12, 32, 8, 128), F32),
        pltpu.VMEM((8, D), F32),
        pltpu.VMEM((8, D), F32),
        pltpu.VMEM((4, 4, ROWS, D), BF16),
        pltpu.VMEM((4, 4, ROWS, D), BF16),
        pltpu.VMEM((2, 3, 40, 256), F32),
        pltpu.VMEM((2, 3, 40, 256), F32),
        pltpu.SemaphoreType.DMA((copies,)),
        pltpu.SemaphoreType.DMA((copies,)),
        pltpu.SemaphoreType.DMA((4,)),
        [Scatter.scratch(D), Scatter.scratch(D), Scatter.scratch(D), Total.scratch(40, 256)],
    ]
    leaves, tree = jax.tree_util.tree_flatten(scratch)
    anywhere = pl.BlockSpec(memory_space=pl.ANY)
    inside = pl.BlockSpec(memory_space=pltpu.VMEM)
    scalar = pl.BlockSpec(memory_space=pltpu.SMEM)
    outs = pl.pallas_call(
        functools.partial(module_kernel, scale, tree),
        out_shape=[
            jax.ShapeDtypeStruct(block, BF16),
            jax.ShapeDtypeStruct(block, BF16),
            jax.ShapeDtypeStruct((ROWS, 2 * D), F32),
            jax.ShapeDtypeStruct((ROWS, D), F32),
            jax.ShapeDtypeStruct((31, D), F32),
            jax.ShapeDtypeStruct((1, D), F32),
            jax.ShapeDtypeStruct((1, D), F32),
        ],
        in_specs=[scalar, anywhere, anywhere, inside, anywhere, inside, inside, anywhere],
        out_specs=[anywhere, anywhere, inside, inside, inside, inside, inside],
        scratch_shapes=leaves,
        compiler_params=pltpu.CompilerParams(
            collective_id=0, has_side_effects=True, vmem_limit_bytes=63 * 2**20
        ),
    )(
        lengths, frames[0], cotangent[0], norm_gain[None], w_in, taps, mid_gain[None], w_out
    )
    mixed, grad_frames, grad_in, grad_out, grad_taps, grad_norm_gain, grad_mid_gain = outs
    return (
        mixed[None], grad_frames[None], grad_in, grad_out,
        grad_taps, grad_norm_gain[0], grad_mid_gain[0],
    )


def solution(mesh):
    return jax.shard_map(
        body,
        mesh=mesh,
        in_specs=(
            P(("utt", "wshard"), "tm", None),
            P(("utt", "wshard")),
            P(("utt", "wshard"), "tm", None),
            P(),
            P(("tm", "wshard"), None),
            P(),
            P(),
            P(("tm", "wshard"), None),
        ),
        out_specs=(
            P(("utt", "wshard"), "tm", None),
            P(("utt", "wshard"), "tm", None),
            P(("tm", "wshard"), None),
            P(("tm", "wshard"), None),
            P(),
            P(),
            P(),
        ),
        check_vma=False,
    )
```

profile of v0, /device:TPU:1, one launch (start us, length us, event | category | flops | bytes accessed | tf_op | source)
XLA Modules:
  0.0 157.0 jit_solution(13943441143644360752)
XLA Ops:
  1.3 1.3 broadcast_in_dim.12.refs_3_
  2.6 1.3 broadcast_in_dim.13.refs_6_
  3.9 1.6 %bitcast_bitcast_fusion.refs_5_ = f32[12,32,128]{2,1,0:T(8,128)} fusion(f32[31,1536]{1,0:T(8,128)} %param.13), kind=kLoop, calls=%fused_computation | loop fusion | bytes 387072 | tf_op jit(solution)/shard_map/transpose | solution.py:864
  5.5 142.4 %shard_map.135 = (bf16[512,1536]{1,0:T(8,128)(2,1)}, bf16[512,1536]{1,0:T(8,128)(2,1)}, f32[48,3072]{1,0:T(8,128)}, f32[48,1536]{1,0:T(8,128)}, f32[31,1536]{1,0...) custom-call(s32[1]{0:T(128)S(6)} %copy.23.refs_0_, bf16[512,1536]{1,0:T(8,128)(2,1)} %bitcast.11, ...), custom_call_target="tpu_custom_call" | custom-call | tf_op jit(solution)/shard_map/pallas_call | solution.py:902
  147.9 1.3 reduce
  149.2 1.3 reduce.1
  150.5 0.0 copy-start
  150.5 2.8 %copy.24 = bf16[1,512,1536]{2,1,0:T(8,128)(2,1)} copy(bf16[1,512,1536]{2,1,0:T(8,128)(2,1)} %bitcast.14) | data formatting | bytes 3145728
  153.3 0.0 copy-done
  153.3 0.0 copy-start.1
  153.3 0.0 copy-start.2
  153.3 1.1 copy.25
  154.5 0.3 copy-done.1
  154.8 0.0 copy-start.3
  154.8 0.8 copy.26
  155.6 0.0 copy-done.2
  155.6 0.7 copy.27
  156.3 0.0 copy-done.3
  156.3 0.7 copy.28
Async XLA Ops:
  150.5 2.8 %copy-start = (bf16[512,1536]{1,0:T(8,128)(2,1)S(1)}, bf16[512,1536]{1,0:T(8,128)(2,1)}, u32[]{:S(2)}) copy-start(bf16[512,1536]{1,0:T(8,128)(2,1)} %get-tuple-element.15) | copy-start | bytes 4718596
  153.3 1.4 copy-start.1
  153.3 2.3 %copy-start.2 = (f32[48,1536]{1,0:T(8,128)S(1)}, f32[48,1536]{1,0:T(8,128)}, u32[]{:S(2)}) copy-start(f32[48,1536]{1,0:T(8,128)} %get-tuple-element.31) | copy-start | bytes 884740
  154.8 1.5 copy-start.3
where the time goes:
time: 157 us
  Pallas kernels  142 us (90%)
  local copies, waits for them, and re-layouts  10.6 us (7%)
  other arithmetic  2.62 us (2%)
    pallas_call x1, Pallas kernels, body(): pl.pallas_call(functools.partial(module_kernel, scale, tree), out_shape=[...  142 us
    unnamed x13, local copies, waits for them, and re-layouts  6.43 us

commit v1 on v0

--- a/solution.py
+++ b/solution.py
@@ -524,7 +524,7 @@
     @pl.loop(0, 12)
     def _(i):
         for base in bases:
-            total = taps_sum(padded, i, base, lambda k: taps[i, k : k + 1, :])
+            total = taps_sum(padded, i, base, lambda k: taps[k : k + 1, rows_of(i, 128)])
             temporal[pl.ds(base, 128), pl.ds(pl.multiple_of(i * 128, 128), 128)] = total
 
 
@@ -561,7 +561,7 @@
         high = pl.ds(pl.multiple_of(D + i * 128, 128), 128)
         for base in range(0, 512, 128):
             rows = pl.ds(base, 128)
-            grad = taps_sum(grad_padded, i, base, lambda k: taps[i, 30 - k : 31 - k, :])
+            grad = taps_sum(grad_padded, i, base, lambda k: taps[30 - k : 31 - k, columns])
             grad = grad * valid(base, 128)
             gate = opened[rows, columns].astype(F32)
             direct = grad * gate
@@ -600,8 +600,8 @@
                 target[rows_of(j, 128), pl.ds(base, 128)] = jnp.transpose(block)
 
 
-def weight_grad(left, right, right_column, target, target_column):
-    @pl.loop(0, 6)
+def weight_grad(first, last, left, right, right_column, target, target_column):
+    @pl.loop(first, last)
     def _(t):
         value = jnp.dot(
             left[...],
@@ -673,14 +673,14 @@
 
 def module_kernel(scale, tree, *refs):
     (
-        length_ref, frames_hbm, cotangent_hbm, norm_gain, in_hbm, taps, mid_gain, out_hbm,
-        mixed_hbm, grad_frames_hbm, grad_in, grad_out, grad_taps, grad_norm_gain, grad_mid_gain,
+        length_ref, frames_hbm, cotangent_hbm, norm_gain_hbm, in_hbm, taps, mid_gain_hbm, out_hbm,
+        mixed_hbm, grad_frames_hbm, grad_in, grad_out, grad_taps, grad_norm_hbm, grad_mid_hbm,
     ) = refs[:15]
     (
         in_full, out_full, frames, branch_grad, normed, smooth, linear, opened, padded, grad_padded,
         temporal, smooth_grad, hidden_grad, normed_t, smooth_t, other_t, mean_ref, inverse_ref,
         sums, mid_term, in_term, first_terms, second_terms, small, small_sum,
-        sent, landed, local, bufs,
+        norm_gain, mid_gain, grad_norm_gain, grad_mid_gain, sent, landed, local, bufs,
     ) = jax.tree_util.tree_unflatten(tree, refs[15:])
     place = Place()
     net = Net(place, sent, landed)
@@ -697,6 +697,8 @@
         pltpu.make_async_copy(frames_hbm, frames, local.at[1]),
         pltpu.make_async_copy(cotangent_hbm, branch_grad.at[0:FRAMES], local.at[2]),
         pltpu.make_async_copy(out_hbm, out_full.at[c, place.y, place.z], local.at[3]),
+        pltpu.make_async_copy(norm_gain_hbm, norm_gain.at[0], local.at[4]),
+        pltpu.make_async_copy(mid_gain_hbm, mid_gain.at[0], local.at[5]),
     ]
     for load in loads:
         load.start()
@@ -705,6 +707,8 @@
     loads[0].wait()
     gather_in.begin()
     loads[1].wait()
+    loads[4].wait()
+    loads[5].wait()
     norm = (frames, norm_gain, normed, mean_ref, inverse_ref)
     norm_stage(0, 6, *norm)
     gather_in.second()
@@ -744,6 +748,14 @@
     net.gone([pair_normed])
     transpose_stage(smooth, smooth_t.at[:, 0:FRAMES], other_t, c)
     pair_smooth = net.send(other_t, smooth_t.at[:, FRAMES : 2 * FRAMES], sibling)
+    branch_stage(smooth, out_full, frames, valid, normed)
+    store_mixed = pltpu.make_async_copy(normed, mixed_hbm, local.at[0])
+    store_mixed.start()
+    net.wait(pair_branch, branch_grad.at[FRAMES : 2 * FRAMES])
+    net.wait(pair_smooth, smooth_t.at[:, FRAMES : 2 * FRAMES])
+    weight_grad(0, 6, smooth_t, branch_grad, lambda t: t * 256, first_terms, lambda t: t * 256)
+    scatter_out = Scatter(net, place, first_terms, bufs[0])
+    scatter_out.step_far()
     arrive()
     conv = (padded, grad_padded, taps, linear, opened, valid, hidden_grad, sums)
     pair_hidden = []
@@ -755,24 +767,14 @@
             there = hidden_grad.at[FRAMES : 2 * FRAMES, column : column + 256]
             pair_hidden.append((net.send(own, there, sibling), there))
 
-    def hidden_arrive():
-        while pair_hidden:
+    def hidden_arrive(groups):
+        for _ in range(2 * groups):
             net.wait(*pair_hidden.pop(0))
 
-    backward(0)
-    net.wait(pair_branch, branch_grad.at[FRAMES : 2 * FRAMES])
-    net.wait(pair_smooth, smooth_t.at[:, FRAMES : 2 * FRAMES])
-    weight_grad(smooth_t, branch_grad, lambda t: t * 256, first_terms, lambda t: t * 256)
-    scatter_out = Scatter(net, place, first_terms, bufs[0])
-    scatter_out.step_far()
-    backward(1)
-    backward(2)
-    scatter_out.step_near()
-    net.wait(pair_normed, normed_t.at[:, FRAMES : 2 * FRAMES])
-    hidden_arrive()
-
-    def grad_half(half, target):
+    def grad_half(first, last, half, target):
         weight_grad(
+            first,
+            last,
             normed_t,
             hidden_grad,
             lambda t: lax.rem(t, 2) * D + half * HALF + lax.div(t, 2) * 256,
@@ -780,27 +782,30 @@
             lambda t: lax.rem(t, 2) * HALF + lax.div(t, 2) * 256,
         )
 
-    grad_half(0, second_terms)
+    third_terms = out_full.at[0]
     scatter_one = Scatter(net, place, second_terms, bufs[1])
+    scatter_two = Scatter(net, place, third_terms, bufs[2])
+    backward(0)
+    backward(1)
+    backward(2)
+    scatter_out.step_near()
+    net.wait(pair_normed, normed_t.at[:, FRAMES : 2 * FRAMES])
+    hidden_arrive(3)
+    grad_half(0, 6, 0, second_terms)
     scatter_one.step_far()
-    scatter_out.step_second()
     backward(3)
-    scatter_out.step_third()
     backward(4)
     scatter_one.step_near()
+    scatter_out.step_second()
     backward(5)
-    scatter_out.step_spread()
-    branch_stage(smooth, out_full, frames, valid, normed)
-    store_mixed = pltpu.make_async_copy(normed, mixed_hbm, local.at[0])
-    store_mixed.start()
+    net.gone(range(out_first, out_last))
+    hidden_arrive(2)
+    grad_half(0, 4, 1, third_terms)
+    hidden_arrive(1)
+    grad_half(4, 6, 1, third_terms)
+    scatter_two.step_far()
+    scatter_out.step_third()
     scatter_one.step_second()
-    hidden_arrive()
-    net.gone(range(out_first, out_last))
-    third_terms = out_full.at[0]
-    grad_half(1, third_terms)
-    scatter_two = Scatter(net, place, third_terms, bufs[2])
-    scatter_two.step_far()
-    scatter_one.step_third()
     reload = pltpu.make_async_copy(cotangent_hbm, opened, local.at[1])
     reload.start()
 
@@ -817,8 +822,10 @@
     own_hidden = hidden_grad.at[0:FRAMES]
     back_product((0, 1), own_hidden, in_full, temporal)
     scatter_two.step_near()
-    back_product((2, 3), own_hidden, in_full, temporal)
-    scatter_two.step_second()
+    back_product((2,), own_hidden, in_full, temporal)
+    scatter_out.step_spread()
+    scatter_one.step_third()
+    back_product((3,), own_hidden, in_full, temporal)
     reload.wait()
     frames_stage(
         frames, opened, norm_gain, mean_ref, inverse_ref, temporal, smooth, in_term
@@ -835,14 +842,15 @@
         small[core, portion, 33:40, lanes] = jnp.zeros((7, 128), F32)
     total = Total(net, place, small, *bufs[3], small_sum)
     total.to_sibling()
-    scatter_two.step_third()
+    scatter_two.step_second()
     total.begin()
     scatter_one.step_spread()
     scatter_out.step_last(store_out)
+    scatter_two.step_third()
     total.step(1)
+    scatter_one.step_last(store_in(0))
     scatter_two.step_spread()
     total.step(2)
-    scatter_one.step_last(store_in(0))
     total.spread()
     scatter_two.step_last(store_in(1))
     total.last()
@@ -852,16 +860,50 @@
             grad_taps[:, columns] = small_sum[core, portion, 0:31, :] * scale
             grad_norm_gain[:, columns] = small_sum[core, portion, 31:32, :] * scale
             grad_mid_gain[:, columns] = small_sum[core, portion, 32:33, :] * scale
+    stores = [
+        pltpu.make_async_copy(grad_norm_gain.at[0], grad_norm_hbm, local.at[4]),
+        pltpu.make_async_copy(grad_mid_gain.at[0], grad_mid_hbm, local.at[5]),
+    ]
+    for store in stores:
+        store.start()
     store_mixed.wait()
     store_frames.wait()
+    for store in stores:
+        store.wait()
     net.drain()
+
+
+def settle_kernel(*refs):
+    count = (len(refs) - 1) // 2
+    copies = [
+        pltpu.make_async_copy(src, dst, refs[-1].at[i])
+        for i, (src, dst) in enumerate(zip(refs[:count], refs[count:-1]))
+    ]
+    for copy in copies:
+        copy.start()
+    for copy in copies:
+        copy.wait()
+
+
+def settle(*arrays):
+    arrays = [a[None] if i < 2 else a for i, a in enumerate(arrays)]
+    inside = pl.BlockSpec(memory_space=pltpu.VMEM)
+    outside = pl.BlockSpec(memory_space=pltpu.HBM)
+    return tuple(
+        pl.pallas_call(
+            settle_kernel,
+            out_shape=[jax.ShapeDtypeStruct(a.shape, a.dtype) for a in arrays],
+            in_specs=[inside] * len(arrays),
+            out_specs=[outside] * len(arrays),
+            scratch_shapes=[pltpu.SemaphoreType.DMA((len(arrays),))],
+        )(*arrays)
+    )
 
 
 def body(frames, lengths, cotangent, norm_gain, w_in, kernel, mid_gain, w_out):
     scale = 1.0 / math.sqrt(
         FRAMES * lax.axis_size("utt") * lax.axis_size("tm") * lax.axis_size("wshard")
     )
-    taps = jnp.pad(kernel, ((0, 1), (0, 0))).reshape(32, 12, 128).swapaxes(0, 1)
     block = (FRAMES, D)
     copies = 2 * GATHER_COPIES + 3 * SCATTER_COPIES + TOTAL_COPIES + 32
     scratch = [
@@ -890,9 +932,13 @@
         pltpu.VMEM((4, 4, ROWS, D), BF16),
         pltpu.VMEM((2, 3, 40, 256), F32),
         pltpu.VMEM((2, 3, 40, 256), F32),
+        pltpu.VMEM((1, D), F32),
+        pltpu.VMEM((1, D), F32),
+        pltpu.VMEM((1, D), F32),
+        pltpu.VMEM((1, D), F32),
         pltpu.SemaphoreType.DMA((copies,)),
         pltpu.SemaphoreType.DMA((copies,)),
-        pltpu.SemaphoreType.DMA((4,)),
+        pltpu.SemaphoreType.DMA((6,)),
         [Scatter.scratch(D), Scatter.scratch(D), Scatter.scratch(D), Total.scratch(40, 256)],
     ]
     leaves, tree = jax.tree_util.tree_flatten(scratch)
@@ -907,23 +953,19 @@
             jax.ShapeDtypeStruct((ROWS, 2 * D), F32),
             jax.ShapeDtypeStruct((ROWS, D), F32),
             jax.ShapeDtypeStruct((31, D), F32),
-            jax.ShapeDtypeStruct((1, D), F32),
-            jax.ShapeDtypeStruct((1, D), F32),
+            jax.ShapeDtypeStruct((D,), F32),
+            jax.ShapeDtypeStruct((D,), F32),
         ],
-        in_specs=[scalar, anywhere, anywhere, inside, anywhere, inside, inside, anywhere],
-        out_specs=[anywhere, anywhere, inside, inside, inside, inside, inside],
+        in_specs=[scalar, anywhere, anywhere, anywhere, anywhere, inside, anywhere, anywhere],
+        out_specs=[anywhere, anywhere, inside, inside, inside, anywhere, anywhere],
         scratch_shapes=leaves,
         compiler_params=pltpu.CompilerParams(
             collective_id=0, has_side_effects=True, vmem_limit_bytes=63 * 2**20
         ),
     )(
-        lengths, frames[0], cotangent[0], norm_gain[None], w_in, taps, mid_gain[None], w_out
+        lengths, frames[0], cotangent[0], norm_gain, w_in, kernel, mid_gain, w_out
     )
-    mixed, grad_frames, grad_in, grad_out, grad_taps, grad_norm_gain, grad_mid_gain = outs
-    return (
-        mixed[None], grad_frames[None], grad_in, grad_out,
-        grad_taps, grad_norm_gain[0], grad_mid_gain[0],
-    )
+    return settle(*outs)
 
 
 def solution(mesh):

time: 157 us -> 141 us (0.90)
  local copies, waits for them, and re-layouts: 10.6 us -> 0 us
  Pallas kernels: 142 us -> 139 us
  other arithmetic: 2.62 us -> 0 us
    pallas_call x1, Pallas kernels: 142 us -> 135 us  [body(): pl.pallas_call(functools.partial(module_kernel, scale, tree), out_shape=[...]
    unnamed x13 -> x0, local copies, waits for them, and re-layouts: 6.43 us -> none
    pallas_call x0 -> x1, Pallas kernels: none -> 4.23 us  [settle(): pl.pallas_call(settle_kernel, out_shape=[jax.ShapeDtypeStruct(a.shape, a....]
    pallas_call x2 -> x0, other arithmetic: 2.62 us -> none  [body(): pl.pallas_call(functools.partial(module_kernel, scale, tree), out_shape=[...]
    broadcast_in_dim x2 -> x0, local copies, waits for them, and re-layouts: 2.59 us -> none  [the longest x1 1.3 us: body(): norm_gain[None]]
    transpose x1 -> x0, local copies, waits for them, and re-layouts: 1.62 us -> none  [body(): taps = jnp.pad(kernel, ((0, 1), (0, 0))).reshape(32, 12, 128).swapaxes(0, 1)]
where the time goes in v1:
time: 141 us; the launch traced here: 140 us
  Pallas kernels  139 us (99%)
  between operations  1.47 us (1%)
    pallas_call x1, Pallas kernels, body(): pl.pallas_call(functools.partial(module_kernel, scale, tree), out_shape=[...  135 us
    pallas_call x1, Pallas kernels, settle(): pl.pallas_call(settle_kernel, out_shape=[jax.ShapeDtypeStruct(a.shape, a....  4.23 us

profile of v1, /device:TPU:1, one launch (start us, length us, event | category | flops | bytes accessed | tf_op | source)
XLA Modules:
  0.0 140.4 jit_solution(17480954337560715715)
XLA Ops:
  1.3 134.7 %shard_map.135 = (bf16[512,1536]{1,0:T(8,128)(2,1)}, bf16[512,1536]{1,0:T(8,128)(2,1)}, f32[48,3072]{1,0:T(8,128)}, f32[48,1536]{1,0:T(8,128)}, f32[31,1536]{1,0:T(8,128)}, /*index=5*/f32[1536]{0:T(1024)}, f32[1536]{0:T(1024)}) custom-call(s32[1]{0:T(128)S(6)} %copy.15.refs_0_, bf16[512,1536]{1,0:T(8,128)(2,1)} %bitcast.6, bf16[512,1536]{1,0:T(8,128)(2,1)} %bitcast.7, ...), custom_call_target="tpu_custom_call" | custom-call | tf_op jit(solution)/shard_map/pallas_call | solution.py:948
  136.0 4.2 %shard_map.136 = (bf16[1,512,1536]{2,1,0:T(8,128)(2,1)}, bf16[1,512,1536]{2,1,0:T(8,128)(2,1)}, f32[48,3072]{1,0:T(8,128)}, f32[48,1536]{1,0:T(8,128)}, f32[31,1...) custom-call(bf16[1,512,1536]{2,1,0:T(8,128)(2,1)} %bitcast.4, bf16[1,512,1536]{2,1,0:T(8,128)(2,1)} %bitcast.5, ...), custom_call_target="tpu_custom_call" | custom-call | tf_op jit(solution)/shard_map/pallas_call | solution.py:893

commit v2 on v1

--- a/solution.py
+++ b/solution.py
@@ -89,7 +89,8 @@
 
     def gone(self, slots):
         for slot in slots:
-            self.flying.pop(slot).wait_send()
+            if slot in self.flying:
+                self.flying.pop(slot).wait_send()
 
     def drain(self):
         self.gone(list(self.flying))
@@ -321,6 +322,15 @@
                     p.at(axis, shift),
                 )
 
+        for which in range(3):
+            axis = self.AXES[which][0]
+            for half, shift in ((0, 1), (1, 3)):
+                self.slots["free", which, half] = net.send(
+                    self.first(which, shift, 1 - half),
+                    self.near[3 + which].at[half, pl.ds(2 - 2 * half, 2)],
+                    p.at(axis, shift),
+                )
+
     def step_near(self):
         net, p = self.net, self.place
         for which in range(3):
@@ -332,8 +342,8 @@
                 for i in range(2):
                     add_into(target.at[i], came.at[i])
                 self.slots["near", which, half] = net.send(
-                    self.first(which, shift),
-                    self.near[3 + which].at[half],
+                    self.first(which, shift, half),
+                    self.near[3 + which].at[half, pl.ds(2 * half, 2)],
                     p.at(axis, shift),
                 )
 
@@ -344,7 +354,8 @@
             target = self.first(which, 0)
             for half in range(2):
                 came = self.near[3 + which].at[half]
-                net.wait(self.slots["near", which, half], came)
+                net.wait(self.slots["free", which, half], came.at[pl.ds(2 - 2 * half, 2)])
+                net.wait(self.slots["near", which, half], came.at[pl.ds(2 * half, 2)])
                 for i in range(4):
                     add_into(target.at[i], came.at[i])
             for shift in (2, 1, 3):
@@ -393,7 +404,7 @@
                 store(which * self.portion + x * self.quarter, self.done[x, which].astype(F32))
 
 
-SCATTER_COPIES = 33
+SCATTER_COPIES = 39
 
 
 class Total:
@@ -542,7 +553,7 @@
         scaled = hat * gain[...]
         s = jax.nn.sigmoid(scaled)
         smooth[rows, :] = swapped((scaled * s).astype(BF16))
-        grad = smooth_grad[rows, :].astype(F32) * (s * (1.0 + scaled * (1.0 - s)))
+        grad = swapped(smooth_grad[rows, :].astype(F32)) * (s * (1.0 + scaled * (1.0 - s)))
         mid_term[...] += jnp.sum((grad * hat).reshape(4, 8, D), 0)
         q = grad * gain[...]
         result = inverse * (
@@ -600,26 +611,24 @@
                 target[rows_of(j, 128), pl.ds(base, 128)] = jnp.transpose(block)
 
 
-def weight_grad(first, last, left, right, right_column, target, target_column):
-    @pl.loop(first, last)
+def weight_grad(left, right, right_column, target):
+    @pl.loop(0, 2)
     def _(t):
-        value = jnp.dot(
-            left[...],
-            right[:, pl.ds(pl.multiple_of(right_column(t), 256), 256)],
-            preferred_element_type=F32,
-        )
-        target[:, :, :, pl.ds(pl.multiple_of(target_column(t), 256), 256)] = (
-            value.astype(BF16).reshape(4, 4, ROWS, 256)
-        )
-
-
-def back_product(parts, left, full, result):
-    for q in parts:
-        yh, c = q // 2, q % 2
-        weights = full[c, 2 * yh : 2 * yh + 2].reshape(384, full.shape[-1])
-        result[:, q * 384 : (q + 1) * 384] = transposed_product(left[...], weights).astype(
-            result.dtype
-        )
+        columns = pl.ds(pl.multiple_of(right_column(t), 256), HALF)
+        for y in range(4):
+            value = jnp.dot(
+                left[y * 192 : y * 192 + 192, :],
+                right[:, columns],
+                preferred_element_type=F32,
+            )
+            target[y, :, :, rows_of(t, HALF)] = value.astype(BF16).reshape(4, ROWS, HALF)
+
+
+def back_product(c, left, full, result):
+    for y in (0, 2):
+        weights = full[c, y : y + 2].reshape(384, full.shape[-1])
+        columns = pl.ds(c * HALF + y * 192, 384)
+        result[:, columns] = transposed_product(left[...], weights).astype(result.dtype)
 
 
 def branch_stage(smooth, out_full, frames, valid, mixed):
@@ -642,7 +651,7 @@
         rows = rows_of(i, 32)
         inverse = inverse_ref[rows, :]
         centred = (frames[rows, :].astype(F32) - mean_ref[rows, :]) * inverse
-        grad = normed_grad[rows, :]
+        grad = swapped(normed_grad[rows, :])
         in_term[...] += jnp.sum((grad * centred).reshape(4, 8, D), 0)
         p = grad * gain[...]
         change = inverse * (
@@ -679,7 +688,7 @@
     (
         in_full, out_full, frames, branch_grad, normed, smooth, linear, opened, padded, grad_padded,
         temporal, smooth_grad, hidden_grad, normed_t, smooth_t, other_t, mean_ref, inverse_ref,
-        sums, mid_term, in_term, first_terms, second_terms, small, small_sum,
+        sums, mid_term, in_term, first_terms, second_terms, small, small_sum, tiny, tiny_sum,
         norm_gain, mid_gain, grad_norm_gain, grad_mid_gain, sent, landed, local, bufs,
     ) = jax.tree_util.tree_unflatten(tree, refs[15:])
     place = Place()
@@ -713,6 +722,9 @@
     norm_stage(0, 6, *norm)
     gather_in.second()
     norm_stage(6, 16, *norm)
+    out_first = net.count
+    loads[3].wait()
+    gather_out.begin()
     gather_in.third()
     loads[2].wait()
 
@@ -724,12 +736,9 @@
     pair_branch = net.send(branch_grad.at[0:FRAMES], branch_grad.at[FRAMES : 2 * FRAMES], sibling)
     transpose_stage(normed, normed_t.at[:, 0:FRAMES], other_t, c)
     pair_normed = net.send(other_t, normed_t.at[:, FRAMES : 2 * FRAMES], sibling)
+    gather_out.second()
     gather_in.fourth()
-    loads[3].wait()
-    out_first = net.count
-    gather_out.begin()
     gather_in.finish()
-    gather_out.second()
     hidden = (normed, in_full, linear, opened, padded, valid)
     hidden_stage(0, 3, *hidden)
     gather_out.third()
@@ -741,7 +750,8 @@
     conv_stage((0, 384), padded, taps, temporal)
     gather_out.finish()
     out_last = net.count
-    back_product(range(4), branch_grad.at[0:FRAMES], out_full, smooth_grad)
+    for core in range(2):
+        back_product(core, branch_grad.at[0:FRAMES], out_full, smooth_grad)
     mid_stage(temporal, mid_gain, smooth_grad, smooth, grad_padded, mid_term)
     arrive = edges(net, place, grad_padded)
 
@@ -753,7 +763,7 @@
     store_mixed.start()
     net.wait(pair_branch, branch_grad.at[FRAMES : 2 * FRAMES])
     net.wait(pair_smooth, smooth_t.at[:, FRAMES : 2 * FRAMES])
-    weight_grad(0, 6, smooth_t, branch_grad, lambda t: t * 256, first_terms, lambda t: t * 256)
+    weight_grad(smooth_t, branch_grad, lambda t: t * HALF, first_terms)
     scatter_out = Scatter(net, place, first_terms, bufs[0])
     scatter_out.step_far()
     arrive()
@@ -771,16 +781,8 @@
         for _ in range(2 * groups):
             net.wait(*pair_hidden.pop(0))
 
-    def grad_half(first, last, half, target):
-        weight_grad(
-            first,
-            last,
-            normed_t,
-            hidden_grad,
-            lambda t: lax.rem(t, 2) * D + half * HALF + lax.div(t, 2) * 256,
-            target,
-            lambda t: lax.rem(t, 2) * HALF + lax.div(t, 2) * 256,
-        )
+    def grad_half(half, target):
+        weight_grad(normed_t, hidden_grad, lambda t: t * D + half * HALF, target)
 
     third_terms = out_full.at[0]
     scatter_one = Scatter(net, place, second_terms, bufs[1])
@@ -791,19 +793,26 @@
     scatter_out.step_near()
     net.wait(pair_normed, normed_t.at[:, FRAMES : 2 * FRAMES])
     hidden_arrive(3)
-    grad_half(0, 6, 0, second_terms)
+    grad_half(0, second_terms)
     scatter_one.step_far()
     backward(3)
     backward(4)
+    backward(5)
+    for i in range(12):
+        lanes = slice((i % 2) * 128, (i % 2) * 128 + 128)
+        columns = slice(i * 128, i * 128 + 128)
+        core, portion = (i // 2) % 2, i // 4
+        small[core, portion, 0:31, lanes] = jnp.sum(sums[i], 1)[0:31]
+        small[core, portion, 31:32, lanes] = jnp.sum(mid_term[:, columns], 0, keepdims=True)
+    total = Total(net, place, small, *bufs[3], small_sum)
+    total.to_sibling()
     scatter_one.step_near()
     scatter_out.step_second()
-    backward(5)
     net.gone(range(out_first, out_last))
-    hidden_arrive(2)
-    grad_half(0, 4, 1, third_terms)
-    hidden_arrive(1)
-    grad_half(4, 6, 1, third_terms)
+    hidden_arrive(3)
+    grad_half(1, third_terms)
     scatter_two.step_far()
+    total.begin()
     scatter_out.step_third()
     scatter_one.step_second()
     reload = pltpu.make_async_copy(cotangent_hbm, opened, local.at[1])
@@ -820,12 +829,13 @@
         return store
 
     own_hidden = hidden_grad.at[0:FRAMES]
-    back_product((0, 1), own_hidden, in_full, temporal)
+    back_product(0, own_hidden, in_full, temporal)
+    total.step(1)
     scatter_two.step_near()
-    back_product((2,), own_hidden, in_full, temporal)
+    back_product(1, own_hidden, in_full, temporal)
+    scatter_one.step_third()
     scatter_out.step_spread()
-    scatter_one.step_third()
-    back_product((3,), own_hidden, in_full, temporal)
+    total.step(2)
     reload.wait()
     frames_stage(
         frames, opened, norm_gain, mean_ref, inverse_ref, temporal, smooth, in_term
@@ -834,32 +844,34 @@
     store_frames.start()
     for i in range(12):
         lanes = slice((i % 2) * 128, (i % 2) * 128 + 128)
-        columns = slice(i * 128, i * 128 + 128)
-        core, portion = (i // 2) % 2, i // 4
-        small[core, portion, 0:31, lanes] = jnp.sum(sums[i], 1)[0:31]
-        small[core, portion, 31:32, lanes] = jnp.sum(in_term[:, columns], 0, keepdims=True)
-        small[core, portion, 32:33, lanes] = jnp.sum(mid_term[:, columns], 0, keepdims=True)
-        small[core, portion, 33:40, lanes] = jnp.zeros((7, 128), F32)
-    total = Total(net, place, small, *bufs[3], small_sum)
-    total.to_sibling()
+        tiny[(i // 2) % 2, i // 4, :, lanes] = in_term[:, i * 128 : i * 128 + 128]
+    rest = Total(net, place, tiny, *bufs[4], tiny_sum)
+    rest.to_sibling()
     scatter_two.step_second()
-    total.begin()
+    rest.begin()
+    total.spread()
     scatter_one.step_spread()
     scatter_out.step_last(store_out)
+    rest.step(1)
     scatter_two.step_third()
-    total.step(1)
     scatter_one.step_last(store_in(0))
+    rest.step(2)
     scatter_two.step_spread()
-    total.step(2)
-    total.spread()
-    scatter_two.step_last(store_in(1))
     total.last()
+    rest.spread()
     for core in range(2):
         for portion in range(3):
             columns = slice(portion * 512 + core * 256, portion * 512 + core * 256 + 256)
             grad_taps[:, columns] = small_sum[core, portion, 0:31, :] * scale
-            grad_norm_gain[:, columns] = small_sum[core, portion, 31:32, :] * scale
-            grad_mid_gain[:, columns] = small_sum[core, portion, 32:33, :] * scale
+            grad_mid_gain[:, columns] = small_sum[core, portion, 31:32, :] * scale
+    scatter_two.step_last(store_in(1))
+    rest.last()
+    for core in range(2):
+        for portion in range(3):
+            columns = slice(portion * 512 + core * 256, portion * 512 + core * 256 + 256)
+            grad_norm_gain[:, columns] = (
+                jnp.sum(tiny_sum[core, portion], 0, keepdims=True) * scale
+            )
     stores = [
         pltpu.make_async_copy(grad_norm_gain.at[0], grad_norm_hbm, local.at[4]),
         pltpu.make_async_copy(grad_mid_gain.at[0], grad_mid_hbm, local.at[5]),
@@ -873,29 +885,38 @@
     net.drain()
 
 
-def settle_kernel(*refs):
-    count = (len(refs) - 1) // 2
-    copies = [
-        pltpu.make_async_copy(src, dst, refs[-1].at[i])
-        for i, (src, dst) in enumerate(zip(refs[:count], refs[count:-1]))
+def settle_kernel(count, *refs):
+    sources, targets, held = refs[:count], refs[count : 2 * count], refs[2 * count : -2]
+    into, out = refs[-2:]
+    first = [
+        pltpu.make_async_copy(src, buf, into.at[i])
+        for i, (src, buf) in enumerate(zip(sources, held))
     ]
-    for copy in copies:
+    second = [
+        pltpu.make_async_copy(buf, dst, out.at[i])
+        for i, (buf, dst) in enumerate(zip(held, targets))
+    ]
+    for copy in first:
         copy.start()
-    for copy in copies:
+    for arrived, copy in zip(first, second):
+        arrived.wait()
+        copy.start()
+    for copy in second:
         copy.wait()
 
 
 def settle(*arrays):
     arrays = [a[None] if i < 2 else a for i, a in enumerate(arrays)]
-    inside = pl.BlockSpec(memory_space=pltpu.VMEM)
+    count = len(arrays)
     outside = pl.BlockSpec(memory_space=pltpu.HBM)
     return tuple(
         pl.pallas_call(
-            settle_kernel,
+            functools.partial(settle_kernel, count),
             out_shape=[jax.ShapeDtypeStruct(a.shape, a.dtype) for a in arrays],
-            in_specs=[inside] * len(arrays),
-            out_specs=[outside] * len(arrays),
-            scratch_shapes=[pltpu.SemaphoreType.DMA((len(arrays),))],
+            in_specs=[outside] * count,
+            out_specs=[outside] * count,
+            scratch_shapes=[pltpu.VMEM(a.shape, a.dtype) for a in arrays]
+            + [pltpu.SemaphoreType.DMA((count,)), pltpu.SemaphoreType.DMA((count,))],
         )(*arrays)
     )
 
@@ -905,7 +926,7 @@
         FRAMES * lax.axis_size("utt") * lax.axis_size("tm") * lax.axis_size("wshard")
     )
     block = (FRAMES, D)
-    copies = 2 * GATHER_COPIES + 3 * SCATTER_COPIES + TOTAL_COPIES + 32
+    copies = 2 * GATHER_COPIES + 3 * SCATTER_COPIES + 2 * TOTAL_COPIES + 32
     scratch = [
         pltpu.VMEM((2, 4, 4, ROWS, 2 * D), BF16),
         pltpu.VMEM((2, 4, 4, ROWS, D), BF16),
@@ -930,8 +951,10 @@
         pltpu.VMEM((8, D), F32),
         pltpu.VMEM((4, 4, ROWS, D), BF16),
         pltpu.VMEM((4, 4, ROWS, D), BF16),
-        pltpu.VMEM((2, 3, 40, 256), F32),
-        pltpu.VMEM((2, 3, 40, 256), F32),
+        pltpu.VMEM((2, 3, 32, 256), F32),
+        pltpu.VMEM((2, 3, 32, 256), F32),
+        pltpu.VMEM((2, 3, 8, 256), F32),
+        pltpu.VMEM((2, 3, 8, 256), F32),
         pltpu.VMEM((1, D), F32),
         pltpu.VMEM((1, D), F32),
         pltpu.VMEM((1, D), F32),
@@ -939,7 +962,7 @@
         pltpu.SemaphoreType.DMA((copies,)),
         pltpu.SemaphoreType.DMA((copies,)),
         pltpu.SemaphoreType.DMA((6,)),
-        [Scatter.scratch(D), Scatter.scratch(D), Scatter.scratch(D), Total.scratch(40, 256)],
+        [Scatter.scratch(D), Scatter.scratch(D), Scatter.scratch(D), Total.scratch(32, 256), Total.scratch(8, 256)],
     ]
     leaves, tree = jax.tree_util.tree_flatten(scratch)
     anywhere = pl.BlockSpec(memory_space=pl.ANY)

time: 141 us -> 144 us (1.021)
  Pallas kernels: 139 us -> 142 us
    pallas_call x1, Pallas kernels: 135 us -> 138 us  [body(): pl.pallas_call(functools.partial(module_kernel, scale, tree), out_shape=[...]
where the time goes in v2:
time: 144 us; the launch traced here: 143 us
  Pallas kernels  142 us (99%)
  between operations  1.47 us (1%)
    pallas_call x1, Pallas kernels, body(): pl.pallas_call(functools.partial(module_kernel, scale, tree), out_shape=[...  138 us
    pallas_call x1, Pallas kernels, settle(): pl.pallas_call(functools.partial(settle_kernel, count), out_shape=[jax.Sh...  3.54 us

profile of v2, /device:TPU:1, one launch (start us, length us, event | category | flops | bytes accessed | tf_op | source)
XLA Modules:
  0.0 143.4 jit_solution(10279819639939182414)
XLA Ops:
  1.3 138.4 %shard_map.135 = (bf16[512,1536]{1,0:T(8,128)(2,1)}, bf16[512,1536]{1,0:T(8,128)(2,1)}, f32[48,3072]{1,0:T(8,128)}, f32[48,1536]{1,0:T(8,128)}, f32[31,1536]{1,0:T(8,128)}, /*index=5*/f32[1536]{0:T(1024)}, f32[1536]{0:T(1024)}) custom-call(s32[1]{0:T(128)S(6)} %copy.15.refs_0_, bf16[512,1536]{1,0:T(8,128)(2,1)} %bitcast.6, bf16[512,1536]{1,0:T(8,128)(2,1)} %bitcast.7, ...), custom_call_target="tpu_custom_call" | custom-call | tf_op jit(solution)/shard_map/pallas_call | solution.py:971
  139.7 3.5 %shard_map.136 = (bf16[1,512,1536]{2,1,0:T(8,128)(2,1)}, bf16[1,512,1536]{2,1,0:T(8,128)(2,1)}, f32[48,3072]{1,0:T(8,128)}, f32[48,1536]{1,0:T(8,128)}, f32[31,1...) custom-call(bf16[1,512,1536]{2,1,0:T(8,128)(2,1)} %bitcast.4, bf16[1,512,1536]{2,1,0:T(8,128)(2,1)} %bitcast.5, ...), custom_call_target="tpu_custom_call" | custom-call | tf_op jit(solution)/shard_map/pallas_call | solution.py:913
